TPU v7x, 32 devices: a whole 2x2x4 slice. The times are simulated.
32 devices in a mesh: groups: 2 (over y), rows: 4 (over z), cols: 4 (over x, core).
Axes of the slice: x: 2, y: 2, z: 4, core: 2. Of those that a mesh axis runs over, the one named last changes fastest.
Arguments:
- iterate: bfloat16 [4096, 2048], P(('groups', 'rows'), 'cols'), parts along dimension 0, may hold values from -6 to 6
- square: bfloat16 [4096, 2048], P(('groups', 'rows'), 'cols'), parts along dimension 0, may hold values from -0.5 to 0.5
- iterate_pattern: int32 [32, 16], P(('groups', 'rows'), 'cols'), parts along dimension 0, may hold values from 0 to 1, as said below
- square_pattern: int32 [32, 16], P(('groups', 'rows'), 'cols'), parts along dimension 0, may hold values from 0 to 1, as said below
- keep_pattern: int32 [32, 16], P(('groups', 'rows'), 'cols'), parts along dimension 0, may hold values 0 or 1
Outputs:
- next_iterate: float32 [4096, 2048], P(('groups', 'rows'), 'cols'), parts along dimension 0
There are 2 independent parts, one for each index of `groups`. A program takes and returns all parts, laid end to end along the dimension named above; each array names one. Nothing has to cross between parts.
Inputs may be any that keep to these rules, and one draw needn't show every extreme that they name: `iterate_pattern`: in each aligned tile of 4 x 4 blocks (block rows k * 4 to k * 4 + 3, block columns likewise) at most 4 blocks are stored, and at least one; some tile holds exactly 4. `square_pattern`: in each aligned tile of 4 x 4 blocks at most 4 blocks are stored, and at least one; some tile holds exactly 4.
All inputs are finite; a program needn't handle non-finite values. No bound on the sum of `keep_pattern` on one device may be relied on, other than what follows from the above.
Results may differ from a plain program's by a relative error of at most 0.0003.
Values may be sent and summed in bfloat16 or wider, within the bound.
A program may use at most 64 MiB of HBM per device.

v0:
```python
import jax
import jax.numpy as jnp
from jax import lax
from jax.sharding import PartitionSpec as P


def expand(values, pattern):
    count = pattern.shape[0]
    block = values.shape[0] // count
    shaped = values.reshape(count, block, count, block)
    shaped = shaped * pattern.astype(values.dtype)[:, None, :, None]
    return shaped.reshape(values.shape)


def per_device(iterate, square, iterate_pattern, square_pattern, keep_pattern):
    sparse_x = expand(iterate, iterate_pattern)
    sparse_sq = expand(square, square_pattern)
    row_panel = lax.all_gather(sparse_x, "cols", axis=1, tiled=True)
    column_panel = lax.all_gather(sparse_sq, "rows", axis=0, tiled=True)
    product = jnp.dot(row_panel, column_panel, preferred_element_type=jnp.float32)
    update = 1.5 * sparse_x.astype(jnp.float32) - 0.5 * product
    return expand(update, keep_pattern)


def solution(mesh):
    return jax.shard_map(
        per_device,
        mesh=mesh,
        in_specs=(
            P(("groups", "rows"), "cols"),
            P(("groups", "rows"), "cols"),
            P(("groups", "rows"), "cols"),
            P(("groups", "rows"), "cols"),
            P(("groups", "rows"), "cols"),
        ),
        out_specs=P(("groups", "rows"), "cols"),
        check_vma=False,
    )
```

profile of v0, /device:TPU:0, one launch (start us, length us, event | category | flops | bytes accessed | tf_op | source)
XLA Modules:
  0.0 92.7 jit_solution(4319100656335028603)
XLA Ops:
  6.5 0.0 copy-start.1
  6.5 0.0 copy-start
  6.5 0.0 all-gather.5.cloned.1.call-start
  6.5 0.7 convert_element_type.14
  7.3 0.2 mul.50
  7.5 0.0 copy-start.2
  7.5 1.9 %bitcast_multiply_fusion = bf16[512,512]{1,0:T(8,128)(2,1)} fusion(bf16[512,512]{1,0:T(8,128)(2,1)} %param.6, bf16[64,8,4,128]{3,2,1,0:T(4,128)(2,1)S(1)} %bitcast.14), kind=kLoop, calls=%fused_computation.3 | loop fusion | flops 262144 | bytes 1572864 | tf_op jit(solution)/shard_map/mul | solution.py:11
  9.4 0.0 all-gather.5.cloned.1.call-update
  9.4 0.0 all-gather.3.cloned.1.call-start
  9.5 0.0 copy-done.1
  9.5 0.2 mul.45
  9.7 0.0 copy-done
  9.7 0.9 bitcast_multiply_fusion.1
  10.6 0.0 all-gather.3.cloned.1.call-update
  10.6 0.0 copy-done.2
  10.7 47.6 %all-gather.5.cloned.1.call-done = bf16[2048,512]{1,0:T(8,128)(2,1)} async-done(((bf16[512,512]{1,0:T(8,128)(2,1)}), bf16[2048,512]{1,0:T(8,128)(2,1)}) %all-gather.5.cloned.1.call-update) | async-done | bytes 2097168 | tf_op jit(solution)/shard_map/all_gather | solution.py:19
  58.2 22.9 %all-gather.3.cloned.1.call-done = bf16[512,2048]{1,0:T(8,128)(2,1)} async-done(((bf16[512,512]{1,0:T(8,128)(2,1)}), bf16[512,2048]{1,0:T(8,128)(2,1)}) %all-gather.3.cloned.1.call-update) | async-done | bytes 2097168 | tf_op jit(solution)/shard_map/all_gather | solution.py:18
  81.1 0.2 mul.55
  81.3 4.5 %fusion.1 = f32[512,512]{1,0:T(8,128)} fusion(bf16[512,2048]{1,0:T(8,128)(2,1)} %all-gather.3.cloned.1.call-done, bf16[2048,512]{1,0:T(8,128)(2,1)} %all-gather.5.cloned.1.call-done, f32[64,8,4,128]{3,2,1,0:T(4,128)S(1)} %bitcast.16, bf16[512,512]{1,0:T(8,128)(2,1)} %bitcast_multiply_fusion.1), kind=kOutput, calls=%fused_computation.2 | convolution fusion | flops 1075052544 | bytes 6815744 | tf_op jit(solution)/shard_map/dot_general | solution.py:20
  (2 shorter events, 0.0 us)
Async XLA Ops:
  6.5 3.0 %copy-start.1 = (s32[4,4]{1,0:T(4,128)S(1)}, s32[4,4]{1,0:T(4,128)}, u32[]{:S(2)}) copy-start(s32[4,4]{1,0:T(4,128)} %param.7) | copy-start | bytes 196
  6.5 3.2 %copy-start = (bf16[512,512]{1,0:T(8,128)(2,1)S(1)}, bf16[512,512]{1,0:T(8,128)(2,1)}, u32[]{:S(2)}) copy-start(bf16[512,512]{1,0:T(8,128)(2,1)} %param.5) | copy-start | bytes 1572868
  6.5 51.7 %all-gather.5.cloned.1.call-start = ((), (), s32[]{:S(2)}) async-start(), calls=%async_computation.1 | async-start | bytes 2621440 | tf_op jit(solution)/shard_map/all_gather | solution.py:19
  7.5 3.2 %copy-start.2 = (s32[4,4]{1,0:T(4,128)S(1)}, s32[4,4]{1,0:T(4,128)}, u32[]{:S(2)}) copy-start(s32[4,4]{1,0:T(4,128)} %param.9) | copy-start | bytes 196
  9.4 71.7 %all-gather.3.cloned.1.call-start = ((), (), s32[]{:S(2)}) async-start(), calls=%async_computation | async-start | bytes 2621440 | tf_op jit(solution)/shard_map/all_gather | solution.py:18
Sparse Core Ops, SparseCore 0:
  9.6 48.6 all-gather.4
  59.8 21.2 all-gather.2
where the time goes:
time: 92.9 us; the launch traced here: 92.7 us
  waiting for transfers between devices  70.5 us (76%)
  between operations  13.5 us (15%)
  matrix products  4.54 us (5%)
  other arithmetic  3.55 us (4%)
    all_gather x1, waiting for transfers between devices, per_device(): column_panel = lax.all_gather(sparse_sq, 'rows', axis=0, tiled=True)  47.6 us
    all_gather x1, waiting for transfers between devices, per_device(): row_panel = lax.all_gather(sparse_x, 'cols', axis=1, tiled=True)  22.9 us
    dot_general x1, matrix products, per_device(): jnp.dot(row_panel, column_panel, preferred_element_type=jnp.float32)  4.54 us
    mul x2, other arithmetic, expand(): shaped = shaped * pattern.astype(values.dtype)[:, None, :, None]  2.8 us
  transfers between devices with their start and end apart: 2, of which 2 were waited for; matrix products, arithmetic and copies ran while one was open for 1% of the time, Pallas kernels for 0%

commit v1 on v0

v1 whole, which is shorter than its diff:
```python
import functools

import jax
import jax.numpy as jnp
from jax import lax
from jax.experimental import pallas as pl
from jax.experimental.pallas import tpu as pltpu
from jax.sharding import PartitionSpec as P

MESH = pl.DeviceIdType.MESH
BLOCKS = 4
MOST = 4
SIZE = 128
CHUNKS = 2
PER = MOST // CHUNKS


def rows_of(i):
    return pl.ds(i * SIZE, SIZE)


def pack(tile_ref, pattern_ref, packed_ref):
    slots = [jnp.zeros((SIZE, SIZE), packed_ref.dtype)] * MOST
    count = jnp.int32(0)
    for b in range(BLOCKS * BLOCKS):
        i, j = b // BLOCKS, b % BLOCKS
        stored = pattern_ref[i, j]
        block = tile_ref[rows_of(i), rows_of(j)]
        for a in range(min(MOST, b + 1)):
            slots[a] = jnp.where((stored > 0) & (count == a), block, slots[a])
        count = count + stored
    for a in range(MOST):
        packed_ref[a] = slots[a]


def unpack(packed_ref, pattern_ref, at, held, dense_ref):
    held[...] = packed_ref[at]
    count = jnp.int32(0)
    for b in range(BLOCKS * BLOCKS):
        i, j = b // BLOCKS, b % BLOCKS
        stored = pattern_ref[at, i, j]
        block = held[jnp.minimum(count, MOST - 1)]
        dense_ref[rows_of(i), rows_of(j)] = jnp.where(stored > 0, block, jnp.zeros_like(block))
        count = count + stored


def kernel(
    nr, nc, xpat_ref, spat_ref, keep_ref, x_ref, s_ref, out_ref,
    xt, st, xp, sp, xh, sh, xd, sd, acc, xpats, spats,
    load_sem, patx_send, patx_recv, pats_send, pats_recv,
    x_send, x_recv, s_up, s_down, s_recv,
):
    r = lax.axis_index("rows")
    c = lax.axis_index("cols")

    load_s = pltpu.make_async_copy(s_ref, st, load_sem.at[0])
    load_x = pltpu.make_async_copy(x_ref, xt, load_sem.at[1])
    load_s.start()
    load_x.start()

    barrier = pltpu.get_barrier_semaphore()
    for d in range(1, nr):
        pl.semaphore_signal(barrier, inc=1, device_id={"rows": lax.rem(r + d, nr)}, device_id_type=MESH)
    for d in range(1, nc):
        pl.semaphore_signal(barrier, inc=1, device_id={"cols": lax.rem(c + d, nc)}, device_id_type=MESH)
    for i in range(BLOCKS):
        for j in range(BLOCKS):
            xpats[c, i, j] = xpat_ref[i, j]
            spats[r, i, j] = spat_ref[i, j]
    load_s.wait()
    pack(st, spat_ref, sp.at[r])
    pl.semaphore_wait(barrier, nr + nc - 2)

    def s_copy(at, chunk, step, sems):
        piece = sp.at[at, pl.ds(chunk * PER, PER)]
        return pltpu.make_async_remote_copy(
            src_ref=piece, dst_ref=piece, send_sem=sems.at[at, chunk], recv_sem=s_recv.at[at, chunk],
            device_id={"rows": r + step}, device_id_type=MESH,
        )

    def pass_on(at, chunk, up, down):
        @pl.when(up)
        def _():
            s_copy(at, chunk, 1, s_up).start()

        @pl.when(down)
        def _():
            s_copy(at, chunk, -1, s_down).start()

    for chunk in range(CHUNKS):
        pass_on(r, chunk, r < nr - 1, r > 0)

    pattern_copies = []
    for d in range(1, nr):
        pattern_copies.append(pltpu.make_async_remote_copy(
            src_ref=spats.at[r], dst_ref=spats.at[r], send_sem=pats_send.at[d], recv_sem=pats_recv.at[d],
            device_id={"rows": lax.rem(r + d, nr)}, device_id_type=MESH))
    for d in range(1, nc):
        pattern_copies.append(pltpu.make_async_remote_copy(
            src_ref=xpats.at[c], dst_ref=xpats.at[c], send_sem=patx_send.at[d], recv_sem=patx_recv.at[d],
            device_id={"cols": lax.rem(c + d, nc)}, device_id_type=MESH))
    for copy in pattern_copies:
        copy.start()

    load_x.wait()
    pack(xt, xpat_ref, xp.at[c])
    x_copies = []
    for d in range(1, nc):
        x_copies.append(pltpu.make_async_remote_copy(
            src_ref=xp.at[c], dst_ref=xp.at[c], send_sem=x_send.at[d], recv_sem=x_recv.at[d],
            device_id={"cols": lax.rem(c + d, nc)}, device_id_type=MESH))
    for copy in x_copies:
        copy.start()

    def multiply(at, first):
        unpack(xp, xpats, at, xh, xd)
        unpack(sp, spats, at, sh, sd)
        half = sd.shape[1] // 2
        for h in range(2):
            part = pl.ds(h * half, half)
            value = jnp.dot(xd[...], sd[:, part], preferred_element_type=jnp.float32)
            acc[:, part] = value if first else acc[:, part] + value

    acc[...] = jnp.zeros_like(acc)
    for copy in pattern_copies:
        copy.wait()
    for copy in x_copies:
        copy.wait()

    def s_step(step, carry):
        below = r - step
        above = r + step
        has_below = (below >= 0) & (step > 0)
        has_above = above < nr

        for chunk in range(CHUNKS):
            @pl.when(has_below)
            def _():
                s_copy(below, chunk, 1, s_up).wait_recv()
                pass_on(below, chunk, r < nr - 1, False)

            @pl.when(has_above & (step > 0))
            def _():
                s_copy(above, chunk, -1, s_down).wait_recv()
                pass_on(above, chunk, False, r > 0)

        def side(k, carry):
            at = jnp.where(k == 0, below, above)

            @pl.when(jnp.where(k == 0, has_below, has_above))
            def _():
                multiply(at, False)
            return carry

        return lax.fori_loop(0, 2, side, carry)

    lax.fori_loop(0, nr, s_step, 0)

    for i in range(BLOCKS):
        for j in range(BLOCKS):
            x = xt[rows_of(i), rows_of(j)].astype(jnp.float32)
            x = jnp.where(xpat_ref[i, j] > 0, x, 0.0)
            update = 1.5 * x - 0.5 * acc[rows_of(i), rows_of(j)]
            out_ref[rows_of(i), rows_of(j)] = jnp.where(keep_ref[i, j] > 0, update, 0.0)

    def drain(at, carry):
        for chunk in range(CHUNKS):
            @pl.when((at <= r) & (r < nr - 1))
            def _():
                s_copy(at, chunk, 1, s_up).wait_send()

            @pl.when((at >= r) & (r > 0))
            def _():
                s_copy(at, chunk, -1, s_down).wait_send()
        return carry

    lax.fori_loop(0, nr, drain, 0)


def per_device(iterate, square, iterate_pattern, square_pattern, keep_pattern, *, nr, nc):
    order = iterate.shape[0]
    smem = pl.BlockSpec(memory_space=pltpu.SMEM)
    anywhere = pl.BlockSpec(memory_space=pl.ANY)
    dma = pltpu.SemaphoreType.DMA
    return pl.pallas_call(
        functools.partial(kernel, nr, nc),
        out_shape=jax.ShapeDtypeStruct(iterate.shape, jnp.float32),
        in_specs=[smem, smem, smem, anywhere, anywhere],
        out_specs=pl.BlockSpec(memory_space=pltpu.VMEM),
        scratch_shapes=[
            pltpu.VMEM((order, order), jnp.bfloat16),
            pltpu.VMEM((order, order), jnp.bfloat16),
            pltpu.VMEM((nc, MOST, SIZE, SIZE), jnp.bfloat16),
            pltpu.VMEM((nr, MOST, SIZE, SIZE), jnp.bfloat16),
            pltpu.VMEM((MOST, SIZE, SIZE), jnp.bfloat16),
            pltpu.VMEM((MOST, SIZE, SIZE), jnp.bfloat16),
            pltpu.VMEM((order, order), jnp.bfloat16),
            pltpu.VMEM((order, order), jnp.bfloat16),
            pltpu.VMEM((order, order), jnp.float32),
            pltpu.SMEM((nc, BLOCKS, BLOCKS), jnp.int32),
            pltpu.SMEM((nr, BLOCKS, BLOCKS), jnp.int32),
            dma((2,)), dma((nc,)), dma((nc,)), dma((nr,)), dma((nr,)),
            dma((nc,)), dma((nc,)), dma((nr, CHUNKS)), dma((nr, CHUNKS)), dma((nr, CHUNKS)),
        ],
        compiler_params=pltpu.CompilerParams(
            collective_id=0, has_side_effects=True, vmem_limit_bytes=60 * 2**20
        ),
        cost_estimate=pl.CostEstimate(
            flops=2 * order * order * order * nr, bytes_accessed=4 * order * order * 2, transcendentals=0
        ),
    )(iterate_pattern, square_pattern, keep_pattern, iterate, square)


def solution(mesh):
    spec = P(("groups", "rows"), "cols")
    return jax.shard_map(
        functools.partial(per_device, nr=mesh.shape["rows"], nc=mesh.shape["cols"]),
        mesh=mesh,
        in_specs=(spec,) * 5,
        out_specs=spec,
        check_vma=False,
    )
```

time: 92.9 us -> 25.5 us (0.27)
  waiting for transfers between devices: 70.5 us -> 0 us
  Pallas kernels: 0 us -> 23 us
  between operations: 13.5 us -> 0.01 us
  matrix products: 4.54 us -> 0 us
  other arithmetic: 3.55 us -> 0 us
  local copies, waits for them, and re-layouts: 0.63 us -> 2.26 us
    all_gather x2 -> x0, waiting for transfers between devices: 70.5 us -> none  [the longest x1 47.6 us: per_device(): column_panel = lax.all_gather(sparse_sq, 'rows', axis=0, tiled=True)]
    pallas_call x0 -> x1, Pallas kernels: none -> 23 us  [per_device(): pl.pallas_call(functools.partial(kernel, nr, nc), out_shape=jax.ShapeDtyp...]
    dot_general x1 -> x0, matrix products: 4.54 us -> none  [per_device(): jnp.dot(row_panel, column_panel, preferred_element_type=jnp.float32)]
    mul x2 -> x0, other arithmetic: 2.8 us -> none  [expand(): shaped = shaped * pattern.astype(values.dtype)[:, None, :, None]]
    unnamed x6 -> x1, local copies, waits for them, and re-layouts: 0.01 us -> 2.26 us
  transfers between devices with their start and end apart: 2 -> 0, of which waited for: 2 -> 0; matrix products, arithmetic and copies ran while one was open for 1% -> 0% of each run, Pallas kernels for 0% -> 0%
where the time goes in v1:
time: 25.5 us; the launch traced here: 25.3 us
  Pallas kernels  23 us (90%)
  local copies, waits for them, and re-layouts  2.26 us (9%)
    pallas_call x1, Pallas kernels, per_device(): pl.pallas_call(functools.partial(kernel, nr, nc), out_shape=jax.ShapeDtyp...  23 us
    unnamed x1, local copies, waits for them, and re-layouts  2.26 us

profile of v1, /device:TPU:0, one launch (start us, length us, event | category | flops | bytes accessed | tf_op | source)
XLA Modules:
  0.0 25.3 jit_solution(13222337554331216053)
XLA Ops:
  0.0 23.0 %shard_map.55 = f32[512,512]{1,0:T(8,128)} custom-call(s32[4,4]{1,0:T(4,128)} %xpat_ref.1, s32[4,4]{1,0:T(4,128)} %spat_ref.1, s32[4,4]{1,0:T(4,128)} %keep_ref.1, bf16[512,512]{1,0:T(8,128)(2,1)} %x_ref.1, bf16[512,512]{1,0:T(8,128)(2,1)} %s_ref.1), custom_call_target="tpu_custom_call" | custom-call | flops 1073741824 | bytes 2097152 | tf_op jit(solution)/shard_map/pallas_call | solution.py:185
  23.0 2.3 %copy.7 = f32[512,512]{1,0:T(8,128)} copy(f32[512,512]{1,0:T(8,128)} %shard_map.55) | data formatting | bytes 2097152

commit v2 on v0

v2 whole, which is shorter than its diff:
```python
import functools

import jax
import jax.numpy as jnp
from jax import lax
from jax.experimental import pallas as pl
from jax.experimental.pallas import tpu as pltpu
from jax.sharding import PartitionSpec as P

MESH = pl.DeviceIdType.MESH
BLOCKS = 4
MOST = 4
SIZE = 128
CODES = BLOCKS * BLOCKS
PACKED = CODES + MOST * SIZE
CUTS = (0, CODES + 2 * SIZE, PACKED)
CHUNKS = len(CUTS) - 1


def rows_of(i):
    return pl.ds(i * SIZE, SIZE)


def pack(tile_ref, pattern_ref, packed_ref):
    row = lax.broadcasted_iota(jnp.int32, (CODES, SIZE), 0)
    codes = jnp.zeros((CODES, SIZE), jnp.int32)
    slots = [jnp.zeros((SIZE, SIZE), packed_ref.dtype)] * MOST
    count = jnp.int32(0)
    for b in range(CODES):
        i, j = b // BLOCKS, b % BLOCKS
        stored = pattern_ref[i, j]
        block = tile_ref[rows_of(i), rows_of(j)]
        for a in range(min(MOST, b + 1)):
            slots[a] = jnp.where((stored > 0) & (count == a), block, slots[a])
        count = count + stored
        codes = jnp.where(row == b, stored * count, codes)
    packed_ref[pl.ds(0, CODES), :] = codes.astype(jnp.float32).astype(packed_ref.dtype)
    for a in range(MOST):
        packed_ref[pl.ds(CODES + a * SIZE, SIZE), :] = slots[a]


def unpack(packed_ref, dense_ref):
    kind = dense_ref.dtype
    codes = packed_ref[pl.ds(0, CODES), :].astype(jnp.float32)
    weights = [jnp.where(codes == a + 1.0, 1.0, 0.0) for a in range(MOST)]
    for b in range(CODES):
        i, j = b // BLOCKS, b % BLOCKS
        block = None
        for a in range(min(MOST, b + 1)):
            weight = jnp.broadcast_to(weights[a][b:b + 1, :], (16, SIZE)).astype(kind)
            slot = packed_ref[pl.ds(CODES + a * SIZE, SIZE), :].reshape(SIZE // 16, 16, SIZE)
            term = slot * weight[None]
            block = term if block is None else block + term
        dense_ref[rows_of(i), rows_of(j)] = block.reshape(SIZE, SIZE)


def kernel(
    nr, nc, xpat_hbm, spat_hbm, keep_hbm, x_hbm, s_hbm, out_hbm,
    xt, st, xp, sp, xd, sd, acc, out, xpat, spat, keep,
    load_sem, out_sem, x_send, x_recv, s_up, s_down, s_recv,
):
    r = lax.axis_index("rows")
    c = lax.axis_index("cols")
    top = r > 0
    bottom = r < nr - 1

    barrier = pltpu.get_barrier_semaphore()

    @pl.when(top)
    def _():
        pl.semaphore_signal(barrier, inc=1, device_id={"rows": r - 1}, device_id_type=MESH)

    @pl.when(bottom)
    def _():
        pl.semaphore_signal(barrier, inc=1, device_id={"rows": r + 1}, device_id_type=MESH)

    for d in range(1, nc):
        pl.semaphore_signal(barrier, inc=1, device_id={"cols": lax.rem(c + d, nc)}, device_id_type=MESH)

    pairs = ((spat_hbm, spat), (s_hbm, st), (xpat_hbm, xpat), (x_hbm, xt), (keep_hbm, keep))
    loads = [pltpu.make_async_copy(a, b, load_sem.at[k]) for k, (a, b) in enumerate(pairs)]
    for load in loads:
        load.start()

    def s_copy(at, chunk, step, sems):
        piece = sp.at[at, pl.ds(CUTS[chunk], CUTS[chunk + 1] - CUTS[chunk])]
        return pltpu.make_async_remote_copy(
            src_ref=piece, dst_ref=piece, send_sem=sems.at[at, chunk], recv_sem=s_recv.at[at, chunk],
            device_id={"rows": r + step}, device_id_type=MESH,
        )

    def pass_on(at, chunk, down, up):
        @pl.when(down)
        def _():
            s_copy(at, chunk, 1, s_down).start()

        @pl.when(up)
        def _():
            s_copy(at, chunk, -1, s_up).start()

    loads[0].wait()
    loads[1].wait()
    pack(st, spat, sp.at[r])
    pl.semaphore_wait(barrier, nc - 1 + top.astype(jnp.int32) + bottom.astype(jnp.int32))
    for chunk in range(CHUNKS):
        pass_on(r, chunk, bottom, top)

    loads[2].wait()
    loads[3].wait()
    pack(xt, xpat, xp.at[c])

    def x_copy(at, to):
        return pltpu.make_async_remote_copy(
            src_ref=xp.at[at], dst_ref=xp.at[at], send_sem=x_send.at[to], recv_sem=x_recv.at[at],
            device_id={"cols": to}, device_id_type=MESH,
        )

    for d in range(1, nc):
        x_copy(c, lax.rem(c + d, nc)).start()

    def arrive(step):
        above = r - step
        below = r + step
        for chunk in range(CHUNKS):
            @pl.when(above >= 0)
            def _():
                s_copy(above, chunk, 1, s_down).wait_recv()
                pass_on(above, chunk, bottom, False)

            @pl.when(below < nr)
            def _():
                s_copy(below, chunk, -1, s_up).wait_recv()
                pass_on(below, chunk, False, top)

    def early(step, carry):
        arrive(step)
        return carry

    lax.fori_loop(1, 3, early, 0)

    def x_tile(at, carry):
        @pl.when(at != c)
        def _():
            x_copy(at, c).wait_recv()

        unpack(xp.at[at], xd.at[at])
        return carry

    lax.fori_loop(0, nc, x_tile, 0)
    acc[...] = jnp.zeros_like(acc)

    def multiply(at):
        unpack(sp.at[at], sd)
        half = sd.shape[1] // 2
        for h in range(2):
            part = pl.ds(h * half, half)
            acc[:, part] += jnp.dot(xd[at], sd[:, part], preferred_element_type=jnp.float32)

    def s_step(step, carry):
        @pl.when(step >= 3)
        def _():
            arrive(step)

        def side(k, carry):
            at = r + (2 * k - 1) * step

            @pl.when((at >= 0) & (at < nr) & (k + step > 0))
            def _():
                multiply(at)
            return carry

        return lax.fori_loop(0, 2, side, carry)

    lax.fori_loop(0, nr, s_step, 0)

    loads[4].wait()
    writes = []
    for i in range(BLOCKS):
        for j in range(BLOCKS):
            x = xt[rows_of(i), rows_of(j)].astype(jnp.float32)
            x = jnp.where(xpat[i, j] > 0, x, 0.0)
            update = 1.5 * x - 0.5 * acc[rows_of(i), rows_of(j)]
            out[rows_of(i), rows_of(j)] = jnp.where(keep[i, j] > 0, update, 0.0)
        writes.append(pltpu.make_async_copy(out.at[rows_of(i)], out_hbm.at[rows_of(i)], out_sem.at[i]))
        writes[-1].start()

    for d in range(1, nc):
        x_copy(c, lax.rem(c + d, nc)).wait_send()

    def drain(at, carry):
        for chunk in range(CHUNKS):
            @pl.when((at <= r) & bottom)
            def _():
                s_copy(at, chunk, 1, s_down).wait_send()

            @pl.when((at >= r) & top)
            def _():
                s_copy(at, chunk, -1, s_up).wait_send()
        return carry

    lax.fori_loop(0, nr, drain, 0)
    for write in writes:
        write.wait()


def per_device(iterate, square, iterate_pattern, square_pattern, keep_pattern, *, nr, nc):
    order = iterate.shape[0]
    anywhere = pl.BlockSpec(memory_space=pl.ANY)
    dma = pltpu.SemaphoreType.DMA
    half = iterate.dtype
    return pl.pallas_call(
        functools.partial(kernel, nr, nc),
        out_shape=jax.ShapeDtypeStruct(iterate.shape, jnp.float32),
        in_specs=[anywhere] * 5,
        out_specs=anywhere,
        scratch_shapes=[
            pltpu.VMEM((order, order), half),
            pltpu.VMEM((order, order), half),
            pltpu.VMEM((nc, PACKED, SIZE), half),
            pltpu.VMEM((nr, PACKED, SIZE), half),
            pltpu.VMEM((nc, order, order), half),
            pltpu.VMEM((order, order), half),
            pltpu.VMEM((order, order), jnp.float32),
            pltpu.VMEM((order, order), jnp.float32),
            pltpu.SMEM((BLOCKS, BLOCKS), jnp.int32),
            pltpu.SMEM((BLOCKS, BLOCKS), jnp.int32),
            pltpu.SMEM((BLOCKS, BLOCKS), jnp.int32),
            dma((5,)), dma((BLOCKS,)), dma((nc,)), dma((nc,)),
            dma((nr, CHUNKS)), dma((nr, CHUNKS)), dma((nr, CHUNKS)),
        ],
        compiler_params=pltpu.CompilerParams(
            collective_id=0, has_side_effects=True, vmem_limit_bytes=60 * 2**20
        ),
        cost_estimate=pl.CostEstimate(
            flops=2 * order * order * order * nr, bytes_accessed=4 * order * order * 2, transcendentals=0
        ),
    )(iterate_pattern, square_pattern, keep_pattern, iterate, square)


def solution(mesh):
    spec = P(("groups", "rows"), "cols")
    return jax.shard_map(
        functools.partial(per_device, nr=mesh.shape["rows"], nc=mesh.shape["cols"]),
        mesh=mesh,
        in_specs=(spec,) * 5,
        out_specs=spec,
        check_vma=False,
    )
```

time: 92.9 us -> 20.9 us (0.22)
  waiting for transfers between devices: 70.5 us -> 0 us
  Pallas kernels: 0 us -> 18.5 us
  between operations: 13.5 us -> 0.01 us
  matrix products: 4.54 us -> 0 us
  other arithmetic: 3.55 us -> 0 us
  local copies, waits for them, and re-layouts: 0.63 us -> 2.26 us
    all_gather x2 -> x0, waiting for transfers between devices: 70.5 us -> none  [the longest x1 47.6 us: per_device(): column_panel = lax.all_gather(sparse_sq, 'rows', axis=0, tiled=True)]
    pallas_call x0 -> x1, Pallas kernels: none -> 18.5 us  [per_device(): pl.pallas_call(functools.partial(kernel, nr, nc), out_shape=jax.ShapeDtyp...]
    dot_general x1 -> x0, matrix products: 4.54 us -> none  [per_device(): jnp.dot(row_panel, column_panel, preferred_element_type=jnp.float32)]
    mul x2 -> x0, other arithmetic: 2.8 us -> none  [expand(): shaped = shaped * pattern.astype(values.dtype)[:, None, :, None]]
    unnamed x6 -> x1, local copies, waits for them, and re-layouts: 0.01 us -> 2.26 us
  transfers between devices with their start and end apart: 2 -> 0, of which waited for: 2 -> 0; matrix products, arithmetic and copies ran while one was open for 1% -> 0% of each run, Pallas kernels for 0% -> 0%
where the time goes in v2:
time: 20.9 us; the launch traced here: 20.8 us
  Pallas kernels  18.5 us (89%)
  local copies, waits for them, and re-layouts  2.26 us (11%)
    pallas_call x1, Pallas kernels, per_device(): pl.pallas_call(functools.partial(kernel, nr, nc), out_shape=jax.ShapeDtyp...  18.5 us
    unnamed x1, local copies, waits for them, and re-layouts  2.26 us

profile of v2, /device:TPU:0, one launch (start us, length us, event | category | flops | bytes accessed | tf_op | source)
XLA Modules:
  0.0 20.8 jit_solution(13083835691442648307)
XLA Ops:
  0.0 18.5 %shard_map.55 = f32[512,512]{1,0:T(8,128)} custom-call(s32[4,4]{1,0:T(4,128)} %xpat_hbm.1, s32[4,4]{1,0:T(4,128)} %spat_hbm.1, s32[4,4]{1,0:T(4,128)} %keep_hbm.1, bf16[512,512]{1,0:T(8,128)(2,1)} %x_hbm.1, bf16[512,512]{1,0:T(8,128)(2,1)} %s_hbm.1), custom_call_target="tpu_custom_call" | custom-call | flops 1073741824 | bytes 2097152 | tf_op jit(solution)/shard_map/pallas_call | solution.py:211
  18.5 2.3 %copy.7 = f32[512,512]{1,0:T(8,128)} copy(f32[512,512]{1,0:T(8,128)} %shard_map.55) | data formatting | bytes 2097152

commit v3 on v2

--- a/solution.py
+++ b/solution.py
@@ -8,13 +8,16 @@
 from jax.sharding import PartitionSpec as P
 
 MESH = pl.DeviceIdType.MESH
+PIECES = 4
 BLOCKS = 4
 MOST = 4
 SIZE = 128
 CODES = BLOCKS * BLOCKS
 PACKED = CODES + MOST * SIZE
-CUTS = (0, CODES + 2 * SIZE, PACKED)
+CUTS = (0, CODES + SIZE, CODES + 2 * SIZE, CODES + 3 * SIZE, PACKED)
 CHUNKS = len(CUTS) - 1
+X_CUTS = (0, PACKED)
+X_CHUNKS = len(X_CUTS) - 1
 
 
 def rows_of(i):
@@ -57,12 +60,19 @@
 def kernel(
     nr, nc, xpat_hbm, spat_hbm, keep_hbm, x_hbm, s_hbm, out_hbm,
     xt, st, xp, sp, xd, sd, acc, out, xpat, spat, keep,
-    load_sem, out_sem, x_send, x_recv, s_up, s_down, s_recv,
+    load_sem, out_sem, x_far, x_near, x_recv, s_up, s_down, s_recv,
 ):
     r = lax.axis_index("rows")
     c = lax.axis_index("cols")
+    chips = nc // 2
+    core = lax.rem(c, 2)
+    chip = lax.div(c, 2)
+    partner = c + 1 - 2 * core
     top = r > 0
     bottom = r < nr - 1
+
+    def same_core(d):
+        return 2 * lax.rem(chip + d, chips) + core
 
     barrier = pltpu.get_barrier_semaphore()
 
@@ -74,12 +84,13 @@
     def _():
         pl.semaphore_signal(barrier, inc=1, device_id={"rows": r + 1}, device_id_type=MESH)
 
-    for d in range(1, nc):
-        pl.semaphore_signal(barrier, inc=1, device_id={"cols": lax.rem(c + d, nc)}, device_id_type=MESH)
+    pl.semaphore_signal(barrier, inc=1, device_id={"cols": partner}, device_id_type=MESH)
+    for d in range(1, chips):
+        pl.semaphore_signal(barrier, inc=1, device_id={"cols": same_core(d)}, device_id_type=MESH)
 
     pairs = ((spat_hbm, spat), (s_hbm, st), (xpat_hbm, xpat), (x_hbm, xt), (keep_hbm, keep))
     loads = [pltpu.make_async_copy(a, b, load_sem.at[k]) for k, (a, b) in enumerate(pairs)]
-    for load in loads:
+    for load in loads[:2]:
         load.start()
 
     def s_copy(at, chunk, step, sems):
@@ -90,18 +101,20 @@
         )
 
     def pass_on(at, chunk, down, up):
+        @pl.when(up)
+        def _():
+            s_copy(at, chunk, -1, s_up).start()
+
         @pl.when(down)
         def _():
             s_copy(at, chunk, 1, s_down).start()
 
-        @pl.when(up)
-        def _():
-            s_copy(at, chunk, -1, s_up).start()
-
     loads[0].wait()
     loads[1].wait()
+    for load in loads[2:]:
+        load.start()
     pack(st, spat, sp.at[r])
-    pl.semaphore_wait(barrier, nc - 1 + top.astype(jnp.int32) + bottom.astype(jnp.int32))
+    pl.semaphore_wait(barrier, chips + top.astype(jnp.int32) + bottom.astype(jnp.int32))
     for chunk in range(CHUNKS):
         pass_on(r, chunk, bottom, top)
 
@@ -109,14 +122,24 @@
     loads[3].wait()
     pack(xt, xpat, xp.at[c])
 
-    def x_copy(at, to):
+    def x_copy(at, chunk, to, send_sem):
+        piece = xp.at[at, pl.ds(X_CUTS[chunk], X_CUTS[chunk + 1] - X_CUTS[chunk])]
         return pltpu.make_async_remote_copy(
-            src_ref=xp.at[at], dst_ref=xp.at[at], send_sem=x_send.at[to], recv_sem=x_recv.at[at],
+            src_ref=piece, dst_ref=piece, send_sem=send_sem, recv_sem=x_recv.at[at, chunk],
             device_id={"cols": to}, device_id_type=MESH,
         )
 
-    for d in range(1, nc):
-        x_copy(c, lax.rem(c + d, nc)).start()
+    def to_far(d, chunk):
+        return x_copy(c, chunk, same_core(d), x_far.at[d, chunk])
+
+    def to_partner(at, chunk):
+        return x_copy(at, chunk, partner, x_near.at[at, chunk])
+
+    for chunk in range(X_CHUNKS):
+        for d in range(1, chips):
+            to_far(d, chunk).start()
+    for chunk in range(X_CHUNKS):
+        to_partner(c, chunk).start()
 
     def arrive(step):
         above = r - step
@@ -132,21 +155,29 @@
                 s_copy(below, chunk, -1, s_up).wait_recv()
                 pass_on(below, chunk, False, top)
 
-    def early(step, carry):
-        arrive(step)
+    between = top & bottom
+    arrive(1)
+
+    @pl.when(between)
+    def _():
+        arrive(2)
+
+    for chunk in range(X_CHUNKS):
+        for d in range(1, chips):
+            to_partner(same_core(d), chunk).wait_recv()
+            to_partner(same_core(d), chunk).start()
+
+    def x_tile(d, carry):
+        mine = same_core(d)
+        other = mine + 1 - 2 * core
+
+        unpack(xp.at[mine], xd.at[mine])
+        for chunk in range(X_CHUNKS):
+            to_partner(other, chunk).wait_recv()
+        unpack(xp.at[other], xd.at[other])
         return carry
 
-    lax.fori_loop(1, 3, early, 0)
-
-    def x_tile(at, carry):
-        @pl.when(at != c)
-        def _():
-            x_copy(at, c).wait_recv()
-
-        unpack(xp.at[at], xd.at[at])
-        return carry
-
-    lax.fori_loop(0, nc, x_tile, 0)
+    lax.fori_loop(0, chips, x_tile, 0)
     acc[...] = jnp.zeros_like(acc)
 
     def multiply(at):
@@ -157,9 +188,11 @@
             acc[:, part] += jnp.dot(xd[at], sd[:, part], preferred_element_type=jnp.float32)
 
     def s_step(step, carry):
-        @pl.when(step >= 3)
+        ahead = step + between.astype(jnp.int32)
+
+        @pl.when(ahead >= 2 + between.astype(jnp.int32))
         def _():
-            arrive(step)
+            arrive(ahead)
 
         def side(k, carry):
             at = r + (2 * k - 1) * step
@@ -184,8 +217,11 @@
         writes.append(pltpu.make_async_copy(out.at[rows_of(i)], out_hbm.at[rows_of(i)], out_sem.at[i]))
         writes[-1].start()
 
-    for d in range(1, nc):
-        x_copy(c, lax.rem(c + d, nc)).wait_send()
+    for chunk in range(X_CHUNKS):
+        for d in range(1, chips):
+            to_far(d, chunk).wait_send()
+        for d in range(chips):
+            to_partner(same_core(d), chunk).wait_send()
 
     def drain(at, carry):
         for chunk in range(CHUNKS):
@@ -199,6 +235,20 @@
         return carry
 
     lax.fori_loop(0, nr, drain, 0)
+    for write in writes:
+        write.wait()
+
+
+def hand_over(from_ref, to_ref, held, sems):
+    size = held.shape[0] // PIECES
+    pieces = [pl.ds(k * size, size) for k in range(PIECES)]
+    reads = [pltpu.make_async_copy(from_ref.at[p], held.at[p], sems.at[0, k]) for k, p in enumerate(pieces)]
+    writes = [pltpu.make_async_copy(held.at[p], to_ref.at[p], sems.at[1, k]) for k, p in enumerate(pieces)]
+    for read in reads:
+        read.start()
+    for read, write in zip(reads, writes):
+        read.wait()
+        write.start()
     for write in writes:
         write.wait()
 
@@ -208,7 +258,7 @@
     anywhere = pl.BlockSpec(memory_space=pl.ANY)
     dma = pltpu.SemaphoreType.DMA
     half = iterate.dtype
-    return pl.pallas_call(
+    result = pl.pallas_call(
         functools.partial(kernel, nr, nc),
         out_shape=jax.ShapeDtypeStruct(iterate.shape, jnp.float32),
         in_specs=[anywhere] * 5,
@@ -225,7 +275,7 @@
             pltpu.SMEM((BLOCKS, BLOCKS), jnp.int32),
             pltpu.SMEM((BLOCKS, BLOCKS), jnp.int32),
             pltpu.SMEM((BLOCKS, BLOCKS), jnp.int32),
-            dma((5,)), dma((BLOCKS,)), dma((nc,)), dma((nc,)),
+            dma((5,)), dma((BLOCKS,)), dma((nc // 2, X_CHUNKS)), dma((nc, X_CHUNKS)), dma((nc, X_CHUNKS)),
             dma((nr, CHUNKS)), dma((nr, CHUNKS)), dma((nr, CHUNKS)),
         ],
         compiler_params=pltpu.CompilerParams(
@@ -235,6 +285,14 @@
             flops=2 * order * order * order * nr, bytes_accessed=4 * order * order * 2, transcendentals=0
         ),
     )(iterate_pattern, square_pattern, keep_pattern, iterate, square)
+    return pl.pallas_call(
+        hand_over,
+        out_shape=jax.ShapeDtypeStruct(iterate.shape, jnp.float32),
+        in_specs=[anywhere],
+        out_specs=anywhere,
+        scratch_shapes=[pltpu.VMEM((order, order), jnp.float32), dma((2, PIECES))],
+        compiler_params=pltpu.CompilerParams(vmem_limit_bytes=60 * 2**20),
+    )(result)
 
 
 def solution(mesh):

time: 20.9 us -> 19.3 us (0.923)
  local copies, waits for them, and re-layouts: 2.26 us -> 0 us
  Pallas kernels: 18.5 us -> 19.2 us
    unnamed x1 -> x0, local copies, waits for them, and re-layouts: 2.26 us -> none
    pallas_call x0 -> x1, Pallas kernels: none -> 1.98 us  [per_device(): pl.pallas_call(hand_over, out_shape=jax.ShapeDtypeStruct(iterate.shape, j...]
    pallas_call x1, Pallas kernels: 18.5 us -> 17.2 us  [per_device(): pl.pallas_call(functools.partial(kernel, nr, nc), out_shape=jax.ShapeDtyp...]
where the time goes in v3:
time: 19.3 us; the launch traced here: 19.2 us
  Pallas kernels  19.2 us (99%)
    pallas_call x1, Pallas kernels, per_device(): pl.pallas_call(functools.partial(kernel, nr, nc), out_shape=jax.ShapeDtyp...  17.2 us
    pallas_call x1, Pallas kernels, per_device(): pl.pallas_call(hand_over, out_shape=jax.ShapeDtypeStruct(iterate.shape, j...  1.98 us

profile of v3, /device:TPU:0, one launch (start us, length us, event | category | flops | bytes accessed | tf_op | source)
XLA Modules:
  0.0 19.2 jit_solution(16164531480918405253)
XLA Ops:
  0.0 17.2 %shard_map.55.from_ref = f32[512,512]{1,0:T(8,128)} custom-call(s32[4,4]{1,0:T(4,128)} %xpat_hbm.1, s32[4,4]{1,0:T(4,128)} %spat_hbm.1, s32[4,4]{1,0:T(4,128)} %keep_hbm.1, bf16[512,512]{1,0:T(8,128)(2,1)} %x_hbm.1, bf16[512,512]{1,0:T(8,128)(2,1)} %s_hbm.1), custom_call_target="tpu_custom_call" | custom-call | flops 1073741824 | bytes 2097152 | tf_op jit(solution)/shard_map/pallas_call | solution.py:261
  17.2 2.0 %shard_map.56 = f32[512,512]{1,0:T(8,128)} custom-call(f32[512,512]{1,0:T(8,128)} %shard_map.55.from_ref), custom_call_target="tpu_custom_call" | custom-call | tf_op jit(solution)/shard_map/pallas_call | solution.py:288

commit v4 on v3

--- a/solution.py
+++ b/solution.py
@@ -8,7 +8,7 @@
 from jax.sharding import PartitionSpec as P
 
 MESH = pl.DeviceIdType.MESH
-PIECES = 4
+PIECES = 2
 BLOCKS = 4
 MOST = 4
 SIZE = 128
@@ -145,15 +145,15 @@
         above = r - step
         below = r + step
         for chunk in range(CHUNKS):
+            @pl.when(below < nr)
+            def _():
+                s_copy(below, chunk, -1, s_up).wait_recv()
+                pass_on(below, chunk, False, top)
+
             @pl.when(above >= 0)
             def _():
                 s_copy(above, chunk, 1, s_down).wait_recv()
                 pass_on(above, chunk, bottom, False)
-
-            @pl.when(below < nr)
-            def _():
-                s_copy(below, chunk, -1, s_up).wait_recv()
-                pass_on(below, chunk, False, top)
 
     between = top & bottom
     arrive(1)
@@ -182,10 +182,7 @@
 
     def multiply(at):
         unpack(sp.at[at], sd)
-        half = sd.shape[1] // 2
-        for h in range(2):
-            part = pl.ds(h * half, half)
-            acc[:, part] += jnp.dot(xd[at], sd[:, part], preferred_element_type=jnp.float32)
+        acc[...] += jnp.dot(xd[at], sd[...], preferred_element_type=jnp.float32)
 
     def s_step(step, carry):
         ahead = step + between.astype(jnp.int32)

time: 19.3 us -> 19.4 us (level)
  no operation moved by 1% of the time
where the time goes in v4:
time: 19.4 us; the launch traced here: 19.2 us
  Pallas kernels  19.2 us (99%)
    pallas_call x1, Pallas kernels, per_device(): pl.pallas_call(functools.partial(kernel, nr, nc), out_shape=jax.ShapeDtyp...  17.2 us
    pallas_call x1, Pallas kernels, per_device(): pl.pallas_call(hand_over, out_shape=jax.ShapeDtypeStruct(iterate.shape, j...  2.04 us

profile of v4, /device:TPU:0, one launch (start us, length us, event | category | flops | bytes accessed | tf_op | source)
XLA Modules:
  0.0 19.2 jit_solution(11353964215273610500)
XLA Ops:
  0.0 17.2 %shard_map.55.from_ref = f32[512,512]{1,0:T(8,128)} custom-call(s32[4,4]{1,0:T(4,128)} %xpat_hbm.1, s32[4,4]{1,0:T(4,128)} %spat_hbm.1, s32[4,4]{1,0:T(4,128)} %keep_hbm.1, bf16[512,512]{1,0:T(8,128)(2,1)} %x_hbm.1, bf16[512,512]{1,0:T(8,128)(2,1)} %s_hbm.1), custom_call_target="tpu_custom_call" | custom-call | flops 1073741824 | bytes 2097152 | tf_op jit(solution)/shard_map/pallas_call | solution.py:258
  17.2 2.0 %shard_map.56 = f32[512,512]{1,0:T(8,128)} custom-call(f32[512,512]{1,0:T(8,128)} %shard_map.55.from_ref), custom_call_target="tpu_custom_call" | custom-call | tf_op jit(solution)/shard_map/pallas_call | solution.py:285
